TPU v7x, 128 devices: a whole 4x4x4 slice. The times are simulated.
128 devices in a mesh: row: 8 (over z, core), col: 16 (over y, x).
Axes of the slice: x: 4, y: 4, z: 4, core: 2. Of those that a mesh axis runs over, the one named last changes fastest.
Arguments:
- descriptors: bfloat16 [32, 262144], P(None, ('row', 'col')), may hold values from -12 to 12
- send_slot: int32 [262144], P(('row', 'col')), may hold values from 0 to 2048, as said below
- recv_slot: int32 [131072], P(('row', 'col')), may hold values from 0 to 2047, as said below
- block_pairs: int32 [2, 131072], P(None, ('row', 'col')), may hold values from 0 to 127, as said below
- start: float32 [16, 1024, 128], P(None, ('row', 'col')), may hold values from -6 to 6
Outputs:
- alphas: float32 [3, 16, 16], replicated
- betas: float32 [3, 16, 16], replicated
- basis: float32 [16, 1024, 128], P(None, ('row', 'col'))
Inputs may be any that keep to these rules, and one draw needn't show every extreme that they name: `send_slot`: A live slot of tile owner s holds d * 16 + k for the block owner d that receives it and its rank k among the segments from s to d; no two live slots of one device share a value; a slot that holds no segment has the value 128 * 16. Every tile owner has some empty slots, and the busiest holds close to twice the mean. The position's segment arrives from device recv_slot // 16 with rank recv_slot % 16; each value of a device's shard is one live send_slot value of that source aimed at this device. `block_pairs`: row 0 is below 128 and row 1 below 64. No pair (I, J) is listed twice, and none has I = J. The list is symmetric: for every listed pair (I, J) the pair (J, I) is listed too, on the device that owns it by the rule of the steps.
All inputs are finite; a program needn't handle non-finite values.
Results may differ from a plain program's by a relative error of at most 0.017.
Values may be sent and summed in bfloat16 or wider, within the bound.
No kernel may reach another device: no remote copies, remote signals or barrier semaphores. Data moves between devices by JAX's collectives and lax.ppermute only.
A program may use at most 64 MiB of HBM per device.

v0:
```python
import functools
import math

import jax
import jax.numpy as jnp
from jax import lax
from jax.experimental import pallas as pl
from jax.experimental.pallas import tpu as pltpu
from jax.sharding import PartitionSpec as P

FEAT = 32
BLOCK = 128
VECS = 16
BUILD_UNROLL = 43
SWEEP_UNROLL = 43
PIECES = 2
EXP2_SCALE = math.log2(math.e) / (2.0 * FEAT)
AXES = ("row", "col")
F32 = jnp.float32
BF16 = jnp.bfloat16
HIGHEST = lax.Precision.HIGHEST
VMEM = pltpu.VMEM


def params(mib):
    return pltpu.CompilerParams(vmem_limit_bytes=mib << 20)


def whole():
    return pl.BlockSpec(memory_space=pltpu.VMEM)


def smem():
    return pl.BlockSpec(memory_space=pltpu.SMEM)


def iota(shape, dim):
    return lax.broadcasted_iota(jnp.int32, shape, dim)


def split3(x):
    high = x.astype(BF16).astype(F32)
    rest = x - high
    middle = rest.astype(BF16).astype(F32)
    low = (rest - middle).astype(BF16).astype(F32)
    return high, middle, low


def dot(left, right):
    return jnp.dot(left, right, precision=HIGHEST, preferred_element_type=F32)


def dot_t(left, right):
    return lax.dot_general(
        left, right, (((1,), (1,)), ((), ())), precision=HIGHEST, preferred_element_type=F32
    )


def encode(small):
    high, middle, low = split3(small)
    return (high + pltpu.roll(middle, 40, 1) + pltpu.roll(low, 80, 1)).astype(BF16)


def decode(tiles):
    total = sum(tiles)
    value = total + pltpu.roll(total, 88, 1) + pltpu.roll(total, 48, 1)
    return jnp.where(iota((VECS, BLOCK), 1) < 40, value, 0.0)


def pad_lanes(small):
    return jnp.concatenate([small, jnp.zeros((VECS, BLOCK - small.shape[1]), F32)], axis=1)


def factor_inverse(gram):
    rows = iota((VECS, BLOCK), 0)
    lanes = iota((VECS, BLOCK), 1)
    work = pad_lanes(gram) + jnp.where(lanes == rows + VECS, 1.0, 0.0)
    columns = [jnp.broadcast_to(work[:, k : k + 1], work.shape) for k in range(VECS)]
    for k in range(VECS):
        inverse = 1.0 / columns[k][k : k + 1, :]
        ratio = jnp.where(rows > k, columns[k], 0.0) * inverse
        for n in range(k + 1, VECS):
            columns[n] = columns[n] - ratio * columns[n][k : k + 1, :]
        work = work - ratio * work[k : k + 1, :]
    diagonal = jnp.sum(jnp.where(lanes == rows, work, 0.0), axis=1, keepdims=True)
    scaled = work * lax.rsqrt(diagonal)
    upper = jnp.where(lanes >= rows, scaled, 0.0)[:, :VECS]
    return upper, scaled[:, VECS : 2 * VECS]


def relay_out_kernel(
    slot_in, desc_in, recv_slot_in, out_ref, recv_slot_out, slot_ref, desc_ref, hot_ref, spread_ref, sems
):
    copies = [
        pltpu.make_async_copy(slot_in, slot_ref, sems.at[0]),
        pltpu.make_async_copy(desc_in, desc_ref, sems.at[1]),
        pltpu.make_async_copy(recv_slot_in, recv_slot_out, sems.at[2]),
    ]
    for copy in copies:
        copy.start()
    for copy in copies:
        copy.wait()
    slots = slot_ref.shape[0] * BLOCK
    rows = out_ref.shape[0]
    target = iota((rows, BLOCK), 0)
    for t in range(slots // BLOCK):
        cut = pl.ds(t * BLOCK, BLOCK)
        slot = slot_ref[t : t + 1, :]
        hot_ref[:, cut] = jnp.where(target == (slot >> 2), 1.0, 0.0).astype(BF16)
        desc = desc_ref[:, cut].astype(F32)
        quarter = slot & 3
        for q in range(4):
            spread_ref[q * FEAT : (q + 1) * FEAT, cut] = jnp.where(quarter == q, desc, 0.0).astype(
                BF16
            )
    out_ref[...] = lax.dot_general(
        hot_ref[...], spread_ref[...], (((1,), (1,)), ((), ())), preferred_element_type=F32
    ).astype(BF16)


def relay_in_kernel(slot_ref, recv_ref, row_ref, own_ref):
    rows = recv_ref.shape[0]
    nblk = slot_ref.shape[0]
    received = recv_ref[...].astype(F32).T.astype(BF16)
    source = iota((rows, BLOCK), 0)
    for b in range(nblk):
        slot = slot_ref[b : b + 1, :]
        hot = jnp.where(source == (slot >> 2), 1.0, 0.0).astype(BF16)
        picked = jnp.dot(received, hot, preferred_element_type=F32)
        quarter = slot & 3
        own = jnp.zeros((FEAT, BLOCK), F32)
        for q in range(4):
            own = own + jnp.where(quarter == q, picked[q * FEAT : (q + 1) * FEAT, :], 0.0)
        own = own.astype(BF16)
        for copy in range(row_ref.shape[0] // nblk):
            row_ref[copy * nblk + b] = own
        own_ref[b] = own


def empty_kernel(*refs):
    for ref in refs[-PIECES:]:
        ref[0, 0:16, 0:BLOCK] = jnp.zeros((16, BLOCK), BF16)


def features(block, sign):
    values = block.astype(F32)
    pieces = split3(jnp.sum(values * values, axis=0, keepdims=True))
    rows = iota((BLOCK - FEAT, BLOCK), 0)
    tail = jnp.zeros((BLOCK - FEAT, BLOCK), F32)
    for n in range(3):
        if sign:
            tail = jnp.where(rows == n, -pieces[n], tail)
            tail = jnp.where(rows == n + 3, 1.0, tail)
        else:
            tail = jnp.where(rows == n, 1.0, tail)
            tail = jnp.where(rows == n + 3, -pieces[n], tail)
    scale = 2.0 if sign else 1.0
    return jnp.concatenate([values * scale, tail], axis=0).astype(BF16)


def each_piece(pieces, body, unroll):
    count = pieces[0].shape[0]

    def step(n, carry):
        for k, weights in enumerate(pieces):
            body(n, carry, weights, k * count)
        return carry

    lax.fori_loop(0, count // unroll, step, 0)


def left_kernel(row_idx, *refs):
    col_desc, left = refs[:-1], refs[-1]
    me = row_idx[row_idx.shape[0] - 1]
    eye = jnp.where(
        iota((BLOCK, BLOCK), 0) == iota((BLOCK, BLOCK), 1), 1.0, 0.0
    ).astype(BF16)
    for m, part in enumerate(col_desc):
        nblk = part.shape[0]
        for k in range(nblk):
            rows = features(part[k], False)
            left[(me ^ m) * nblk + k] = lax.dot_general(
                eye, rows, (((1,), (1,)), ((), ())), preferred_element_type=F32
            ).astype(BF16)


def build_kernel(row_idx, col_idx, row_desc, left, *refs, unroll):
    pieces = refs[PIECES : 2 * PIECES]
    degree, right, total = refs[2 * PIECES :]
    nrow = row_desc.shape[0]

    def prepare_row(n, carry):
        for k in range(8):
            right[n * 8 + k] = features(row_desc[n * 8 + k], True)
            total[n * 8 + k] = jnp.zeros((8, BLOCK), F32)
        return carry

    lax.fori_loop(0, nrow // 8, prepare_row, 0)

    def several(step, carry, weights, first):
        for u in range(unroll):
            group = step * unroll + u
            for q in range(4):
                i = row_idx[(first + group) * 4 + q]
                j = col_idx[(first + group) * 4 + q]
                power = jnp.dot(left[j], right[i], preferred_element_type=F32)
                block = jnp.exp2(power * EXP2_SCALE).astype(BF16)
                r, c = q // 2, q % 2
                weights[group, r * BLOCK : (r + 1) * BLOCK, c * BLOCK : (c + 1) * BLOCK] = block
                total[i] += jnp.sum(block.astype(F32).reshape(BLOCK // 8, 8, BLOCK), axis=0)
        return carry

    each_piece(pieces, several, unroll)
    for n in range(nrow):
        degree[n // 8, n % 8 : n % 8 + 1, :] = jnp.sum(total[n], axis=0, keepdims=True)


def sweep_kernel(row_idx, col_idx, *refs, unroll, peers):
    pieces = refs[:PIECES]
    parts = refs[PIECES : PIECES + peers]
    out, vectors, total = refs[PIECES + peers :]
    me = row_idx[row_idx.shape[0] - 1]
    for m in range(peers):
        for b in range(9):
            vectors[(me ^ m) * 9 + b] = parts[m][b]
    total[...] = jnp.zeros_like(total)
    zero = jnp.zeros((VECS, BLOCK), BF16)

    def several(step, carry, weights, first):
        for u in range(unroll):
            group = step * unroll + u
            picked = [vectors[col_idx[(first + group) * 4 + q]] for q in range(4)]
            lhs = jnp.concatenate(
                [
                    jnp.concatenate([picked[0], zero], 1),
                    jnp.concatenate([zero, picked[2]], 1),
                    jnp.concatenate([picked[1], zero], 1),
                    jnp.concatenate([zero, picked[3]], 1),
                ],
                0,
            )
            result = jnp.dot(lhs, weights[group], preferred_element_type=F32)
            for place, q in enumerate((0, 2, 1, 3)):
                half = (q % 2) * BLOCK
                total[row_idx[(first + group) * 4 + q]] += result[
                    place * VECS : (place + 1) * VECS, half : half + BLOCK
                ]
        return carry

    each_piece(pieces, several, unroll)
    small = encode(decode([part[8].astype(F32) for part in parts]))
    for n in range(total.shape[0]):
        out[n // 8, n % 8] = total[n].astype(BF16)
    for p in range(out.shape[0]):
        out[p, 8] = small


def row_vector(block):
    return jnp.concatenate([block[b : b + 1, :] for b in range(8)], axis=1)


def send(out, vectors, small):
    tile = encode(small)
    for b in range(8):
        out[b] = vectors[:, b * BLOCK : (b + 1) * BLOCK].astype(BF16)
    out[8] = tile


def receive(recv):
    peers = recv.shape[0]
    tiles = []
    for b in range(8):
        tile = recv[0, b].astype(F32)
        for p in range(1, peers):
            tile = tile + recv[p, b].astype(F32)
        tiles.append(tile)
    return jnp.concatenate(tiles, axis=1), decode([recv[p, 8].astype(F32) for p in range(peers)])


def stacked(parts):
    width = parts[0].shape[1]
    return jnp.concatenate(parts + [jnp.zeros((7, width), F32)], axis=0)


def scale_kernel(degree_ref, start_ref, out, degree_out, start_out):
    degree = degree_ref[0]
    for p in range(1, degree_ref.shape[0]):
        degree = degree + degree_ref[p]
    flat = row_vector(degree)
    scale = lax.rsqrt(flat)
    start = jnp.concatenate([start_ref[:, b, :] for b in range(8)], axis=1)
    degree_out[...] = flat
    start_out[...] = start
    root = jnp.sqrt(flat)
    small = pad_lanes(dot_t(start, stacked([start, jnp.zeros_like(start), root])))
    whole_sum = jnp.sum(flat, axis=1, keepdims=True)
    first = (iota((VECS, BLOCK), 0) == 0) & (iota((VECS, BLOCK), 1) == 33)
    small = small + jnp.where(first, whole_sum, 0.0)
    send(out, start * scale, small)


def first_kernel(recv, degree_ref, start_ref, out, basis_out, image_out, trivial_out):
    swept, small = receive(recv)
    degree = degree_ref[...]
    scale = lax.rsqrt(degree)
    total = small[0:1, 33:34]
    trivial = jnp.sqrt(degree / total)
    coef = small[:, 32:33] * lax.rsqrt(total)
    lanes = iota((VECS, BLOCK), 1)
    wide = jnp.where(lanes == 0, coef, 0.0)
    gram = small[:, :VECS] - dot_t(wide, wide)
    upper, inverse = factor_inverse(gram)
    along = coef * trivial
    both = dot(
        inverse,
        jnp.concatenate([start_ref[...] - along, swept * scale - along], axis=1),
    )
    width = degree.shape[1]
    basis, image = both[:, :width], both[:, width:]
    basis_out[...] = basis
    image_out[...] = image
    trivial_out[...] = trivial
    send(out, image * scale, pad_lanes(dot_t(image, stacked([basis, image, trivial]))))


def second_kernel(
    recv, degree_ref, trivial_ref, basis_ref, image_ref, out, basis_out, image_out, rest_out, mats
):
    swept, small = receive(recv)
    scale = lax.rsqrt(degree_ref[...])
    trivial = trivial_ref[...]
    alpha_t = small[:, :VECS]
    gram = small[:, VECS : 2 * VECS] - dot_t(alpha_t, alpha_t)
    upper, inverse = factor_inverse(gram)
    width = trivial.shape[1]
    mixed = dot(alpha_t, jnp.concatenate([basis_ref[...], image_ref[...]], axis=1))
    residual = image_ref[...] - mixed[:, :width]
    applied = swept * scale - small[:, 2 * VECS : 2 * VECS + 1] * trivial - mixed[:, width:]
    both = dot(inverse, jnp.concatenate([residual, applied], axis=1))
    basis, image = both[:, :width], both[:, width:]
    rest = image - dot(upper, basis_ref[...])
    basis_out[...] = basis
    image_out[...] = image
    rest_out[...] = rest
    mats[0] = alpha_t
    mats[1] = upper
    send(out, rest * scale, pad_lanes(dot_t(rest, stacked([basis, rest, trivial]))))


def third_kernel(
    recv, degree_ref, trivial_ref, basis_ref, image_ref, rest_ref, out, basis_out, rest_out, mats
):
    swept, small = receive(recv)
    scale = lax.rsqrt(degree_ref[...])
    trivial = trivial_ref[...]
    alpha_t = small[:, :VECS]
    gram = small[:, VECS : 2 * VECS] - dot_t(alpha_t, alpha_t)
    upper, inverse = factor_inverse(gram)
    width = trivial.shape[1]
    mixed = dot(alpha_t, jnp.concatenate([basis_ref[...], image_ref[...]], axis=1))
    residual = rest_ref[...] - mixed[:, :width]
    applied = swept * scale - small[:, 2 * VECS : 2 * VECS + 1] * trivial - mixed[:, width:]
    both = dot(inverse, jnp.concatenate([residual, applied], axis=1))
    basis, image = both[:, :width], both[:, width:]
    rest = image - dot(upper, basis_ref[...])
    basis_out[...] = basis
    rest_out[...] = rest
    mats[0] = alpha_t
    mats[1] = upper
    small = pad_lanes(
        dot_t(rest, jnp.concatenate([basis, rest], axis=0))
    )
    packed = small[0:4, :]
    for q in range(1, 4):
        packed = packed + pltpu.roll(small[4 * q : 4 * q + 4, :], 32 * q, 1)
    tile = jnp.concatenate([packed] * 4, axis=0).astype(BF16)
    for p in range(out.shape[0] // 16):
        out[p * 16 : (p + 1) * 16, :] = tile


def last_kernel(recv, basis_ref, rest_ref, mats_a, mats_b, alphas, betas, out, *, norm):
    tile = recv[0:16, :].astype(F32)
    for p in range(1, recv.shape[0] // 16):
        tile = tile + recv[p * 16 : (p + 1) * 16, :].astype(F32)
    packed = tile[0:4, :] + tile[4:8, :] + tile[8:12, :] + tile[12:16, :]
    lanes = iota((4, BLOCK), 1)
    rows = []
    for q in range(4):
        part = packed if q == 0 else pltpu.roll(packed, BLOCK - 32 * q, 1)
        rows.append(jnp.where(lanes < 32, part, 0.0))
    small = jnp.concatenate(rows, axis=0)
    alpha_t = small[:, :VECS]
    gram = small[:, VECS : 2 * VECS] - dot_t(alpha_t, alpha_t)
    upper, inverse = factor_inverse(gram)
    final = dot(inverse * norm, rest_ref[...] - dot(alpha_t, basis_ref[...]))
    for b in range(8):
        out[:, b, :] = final[:, b * BLOCK : (b + 1) * BLOCK]
    alphas[0] = mats_a[0].T
    alphas[1] = mats_b[0].T
    alphas[2] = alpha_t.T
    betas[0] = mats_a[1]
    betas[1] = mats_b[1]
    betas[2] = upper


def call(kernel, out_shape, mib, *args, scratch=(), specs=None, out_specs=None, aliases=None):
    outs = out_shape if isinstance(out_shape, (list, tuple)) else None
    return pl.pallas_call(
        kernel,
        out_shape=out_shape,
        in_specs=specs or [whole()] * len(args),
        out_specs=out_specs or ([whole()] * len(outs) if outs else whole()),
        scratch_shapes=list(scratch),
        input_output_aliases=aliases or {},
        compiler_params=params(mib),
    )(*args)


def exchange(values, axis):
    return lax.all_to_all(values, axis, split_axis=0, concat_axis=0, tiled=True)


def column_parts(own, rows):
    parts = [own] + [toggled(own, m, rows) for m in range(2, rows, 2)]
    return [p for part in parts for p in (part, toggled(part, 1, rows))]


def toggled(values, bits, size):
    return lax.ppermute(values, "row", [(i, i ^ bits) for i in range(size)])


def shape(dims, dtype=F32):
    return jax.ShapeDtypeStruct(dims, dtype)


def on_device(descriptors, send_slot, recv_slot, block_pairs, start):
    rows = lax.axis_size("row")
    cols = lax.axis_size("col")
    count = rows * cols
    feat, slots = descriptors.shape
    seg = recv_slot.shape[0]
    nblk = seg // BLOCK
    nrow, ncol = cols * nblk, rows * nblk
    own = jnp.arange(nblk, dtype=jnp.int32)
    me = lax.axis_index("row")
    row_idx = jnp.concatenate([block_pairs[0], lax.axis_index("col") * nblk + own, me[None]])
    col_idx = jnp.concatenate([block_pairs[1], me * nblk + own])
    skip_idx = col_idx + col_idx // nblk
    groups = col_idx.shape[0] // 4
    build_unroll = math.gcd(BUILD_UNROLL, groups // PIECES)
    sweep_unroll = math.gcd(SWEEP_UNROLL, groups // PIECES)

    with jax.named_scope("relay"):
        packed_rows = slots // 4
        outgoing, slots_in = call(
            relay_out_kernel,
            [shape((packed_rows, BLOCK), BF16), shape((nblk, BLOCK), jnp.int32)],
            16,
            pltpu.with_memory_space_constraint(send_slot.reshape(slots // BLOCK, BLOCK), pltpu.HBM),
            pltpu.with_memory_space_constraint(descriptors, pltpu.HBM),
            pltpu.with_memory_space_constraint(recv_slot.reshape(nblk, BLOCK), pltpu.HBM),
            scratch=[
                VMEM((slots // BLOCK, BLOCK), jnp.int32),
                VMEM((feat, slots), BF16),
                VMEM((packed_rows, slots), BF16),
                VMEM((BLOCK, slots), BF16),
                pltpu.SemaphoreType.DMA((3,)),
            ],
            specs=[pl.BlockSpec(memory_space=pltpu.HBM)] * 3,
        )
        received = exchange(outgoing, AXES)
        row_copies, own_desc = call(
            relay_in_kernel,
            [shape((nrow, FEAT, BLOCK), BF16), shape((nblk, FEAT, BLOCK), BF16)],
            16,
            slots_in,
            received,
        )
    with jax.named_scope("gather"):
        row_desc = exchange(row_copies, "col")
        left = call(
            left_kernel,
            shape((ncol, BLOCK, BLOCK), BF16),
            4,
            row_idx,
            *column_parts(own_desc, rows),
            specs=[smem()] + [whole()] * rows,
        )
    with jax.named_scope("build"):
        wshape = pltpu.VMEM((groups // PIECES, 2 * BLOCK, 2 * BLOCK), BF16)
        empty = call(
            empty_kernel,
            [wshape] * PIECES,
            1,
            row_desc,
            left,
            row_idx,
            col_idx,
            skip_idx,
            specs=[pl.BlockSpec(memory_space=pl.ANY)] * 5,
        )
        empty = [pltpu.with_memory_space_constraint(piece, pltpu.VMEM) for piece in empty]
        *weights, degree_part = call(
            functools.partial(build_kernel, unroll=build_unroll),
            [wshape] * PIECES + [shape((cols, nblk, BLOCK))],
            8,
            row_idx,
            col_idx,
            row_desc,
            left,
            *empty,
            scratch=[
                VMEM((nrow, BLOCK, BLOCK), BF16),
                VMEM((nrow, 8, BLOCK), F32),
            ],
            specs=[smem(), smem(), whole(), whole()] + [pl.BlockSpec(memory_space=pl.ANY)] * PIECES,
            aliases={4 + k: k for k in range(PIECES)},
        )
        weights = [pltpu.with_memory_space_constraint(piece, pltpu.VMEM) for piece in weights]
    with jax.named_scope("degree"):
        sent, degree, begin = call(
            scale_kernel,
            [shape((9, VECS, BLOCK), BF16), shape((1, seg)), shape((VECS, seg))],
            8,
            exchange(degree_part, "col"),
            start,
        )

    def sweep(sent):
        vectors = column_parts(sent, rows)
        partial_sum = call(
            functools.partial(sweep_kernel, unroll=sweep_unroll, peers=rows),
            shape((cols, 9, VECS, BLOCK), BF16),
            8,
            row_idx,
            skip_idx,
            *weights,
            *vectors,
            scratch=[VMEM((rows * 9, VECS, BLOCK), BF16), VMEM((nrow, VECS, BLOCK), F32)],
            specs=[smem(), smem()] + [whole()] * (PIECES + rows),
        )
        return exchange(partial_sum, "col")

    vec = shape((VECS, seg))
    sending = shape((9, VECS, BLOCK), BF16)
    mats = shape((2, VECS, VECS))
    with jax.named_scope("step0"):
        swept = sweep(sent)
        sent, basis0, image0, trivial = call(
            first_kernel, [sending, vec, vec, shape((1, seg))], 8, swept, degree, begin
        )
    with jax.named_scope("step1"):
        swept = sweep(sent)
        sent, basis1, image1, rest1, mats0 = call(
            second_kernel, [sending, vec, vec, vec, mats], 8, swept, degree, trivial, basis0, image0
        )
    with jax.named_scope("step2"):
        swept = sweep(sent)
        small, basis2, rest2, mats1 = call(
            third_kernel,
            [shape((count * 4, BLOCK), BF16), vec, vec, mats],
            8,
            swept,
            degree,
            trivial,
            basis1,
            image1,
            rest1,
        )
    with jax.named_scope("finish"):
        three = shape((3, VECS, VECS))
        return tuple(
            call(
                functools.partial(last_kernel, norm=math.sqrt(count * seg)),
                [three, three, shape((VECS, nblk, BLOCK))],
                8,
                exchange(small, AXES),
                basis2,
                rest2,
                mats0,
                mats1,
            )
        )


def solution(mesh):
    return jax.shard_map(
        on_device,
        mesh=mesh,
        in_specs=(
            P(None, ("row", "col")),
            P(("row", "col")),
            P(("row", "col")),
            P(None, ("row", "col")),
            P(None, ("row", "col"), None),
        ),
        out_specs=(P(), P(), P(None, ("row", "col"), None)),
        check_vma=False,
    )
```

profile of v0, /device:TPU:1, one launch (start us, length us, event | category | flops | bytes accessed | tf_op | source)
XLA Modules:
  0.0 188.9 jit_solution(4105373308386100502)
XLA Ops:
  0.6 2.0 %relay.2 = (bf16[512,128]{1,0:T(8,128)(2,1)S(1)}, s32[8,128]{1,0:T(8,128)S(1)}) custom-call(s32[16,128]{1,0:T(8,128)} %bitcast.15, bf16[32,2048]{1,0:T(8,128)(2,1)} %desc_in.1, s32[8,128]{1,0:T(8,128)} %bitcast.16), custom_call_target="tpu_custom_call" | custom-call | tf_op jit(solution)/shard_map/relay/pallas_call | solution.py:408
  2.7 21.5 %all_to_all.47 = bf16[128,4,128]{2,1,0:T(4,128)(2,1)S(1)} all-to-all(bf16[128,4,128]{2,1,0:T(4,128)(2,1)S(1)} %bitcast.12), channel_id=1, replica_groups=mesh['row'=8,'col'=16] {'row','col'}, dimensions={0} | all-to-all | bytes 262144 | tf_op jit(solution)/shard_map/relay/all_to_all | solution.py:420
  24.2 1.5 relay.3
  25.7 3.7 %all-to-all-start.1 = ((bf16[128,32,128]{2,1,0:T(8,128)(2,1)}), bf16[128,32,128]{2,1,0:T(8,128)(2,1)S(1)}, u32[]{:S(2)}, u32[]{:S(2)}) async-start(bf16[128,32,128]{2,1,0:T(8,128)(2,1)} %get-tuple-element.30), calls=%async_computation.1 | async-start | bytes 2097152 | tf_op jit(solution)/shard_map/gather/all_to_all | solution.py:420
  29.4 0.8 fusion.3
  30.3 0.6 collective-permute-start.5
  30.9 1.7 collective-permute-start.3
  32.6 0.9 collective-permute-start.1
  33.5 1.5 collective-permute-start
  35.1 1.8 collective-permute-start.6
  36.9 0.7 collective-permute-start.4
  37.7 0.5 collective-permute-start.2
  38.6 0.5 collective-permute-done.2.refs_3_
  39.1 1.3 gather.1.refs_1_.left
  40.4 5.2 %all-to-all-done.1.refs_0_.row_desc = bf16[128,32,128]{2,1,0:T(8,128)(2,1)S(1)} async-done(((bf16[128,32,128]{2,1,0:T(8,128)(2,1)}), bf16[128,32,128]{2,1,0:T(8,128)(2,1)S(1)}, u32[]{:S(2)}, u32[]{:S(2)}) %all-to-all-start.1) | async-done | bytes 1048608 | tf_op jit(solution)/shard_map/gather/all_to_all | solution.py:420
  45.6 15.5 %build.3 = (bf16[129,256,256]{2,1,0:T(8,128)(2,1)S(1)}, bf16[129,256,256]{2,1,0:T(8,128)(2,1)S(1)}, f32[16,8,128]{2,1,0:T(8,128)S(1)}) custom-call(s32[1033]{0:T(1024)S(1)} %concatenate.6.row_idx.refs_2_, s32[1032]{0:T(1024)S(1)} %get-tuple-element.55.refs_3_.col_idx, ...), custom_call_target="tpu_custom_call", output_to_operand_aliasing={{0}: (4, {}), {1}: (5, {})} | custom-call | tf_op jit(solution)/shard_map/build/pallas_call | solution.py:408
  61.1 10.8 %all_to_all.48.degree_ref = f32[16,8,128]{2,1,0:T(8,128)S(1)} all-to-all(f32[16,8,128]{2,1,0:T(8,128)S(1)} %get-tuple-element.36), channel_id=1, replica_groups=mesh['row'=8,'col'=16] {'col'}, dimensions={0} | all-to-all | bytes 131072 | tf_op jit(solution)/shard_map/degree/all_to_all | solution.py:420
  72.3 0.7 collective-permute-start.12
  72.9 1.7 collective-permute-start.10
  74.7 0.9 collective-permute-start.8
  75.5 2.8 %collective-permute-start.7 = (bf16[9,16,128]{2,1,0:T(8,128)(2,1)S(1)}, bf16[9,16,128]{2,1,0:T(8,128)(2,1)S(1)}, u32[]{:S(2)}, u32[]{:S(2)}) collective-permute-start(bf16[9,16,128]{2,1,0:T(8,128)(2,1)S(1)} %get-tuple-element.37.refs_2_), channel_id=1, source_target_pairs={{0,16},{16,0},{32,48},{48,32},{64,80},{80,64},{96,112},{112,96},{1... | collective-permute-start | bytes 110600 | tf_op jit(solution)/shard_map/step0/ppermute | solution.py:429
  78.3 1.1 collective-permute-start.13
  79.4 1.2 collective-permute-start.11
  81.9 7.2 %step0.2 = bf16[16,9,16,128]{3,2,1,0:T(8,128)(2,1)S(1)} custom-call(s32[1033]{0:T(1024)S(1)} %concatenate.6.row_idx.refs_2_, s32[1032]{0:T(1024)S(1)} %get-tuple-element.56.refs_4_.col_idx, bf16[129,256,256]{2,1,0:T(8,128)(2,1)S(1)} %get-tuple-element.34.refs_0_, bf16[129,256,256]{2,1,0:T(8,128)(2,1)S(1)} %get-tuple-element.35.refs_1_, ...), custom_call_target="tpu_custom_call" | custom-call | tf_op jit(solution)/shard_map/step0/pallas_call | solution.py:408
  89.1 14.2 %all_to_all.49.recv = bf16[16,9,16,128]{3,2,1,0:T(8,128)(2,1)S(1)} all-to-all(bf16[16,9,16,128]{3,2,1,0:T(8,128)(2,1)S(1)} %step0.2), channel_id=1, replica_groups=mesh['row'=8,'col'=16] {'col'}, dimensions={0} | all-to-all | bytes 1179648 | tf_op jit(solution)/shard_map/step0/all_to_all | solution.py:420
  103.3 1.4 step0.3
  104.7 2.2 %collective-permute-start.19 = (bf16[9,16,128]{2,1,0:T(8,128)(2,1)S(1)}, bf16[9,16,128]{2,1,0:T(8,128)(2,1)S(1)}, u32[]{:S(2)}, u32[]{:S(2)}) collective-permute-start(bf16[9,16,128]{2,1,0:T(8,128)(2,1)S(1)} %get-tuple-element.40.refs_2_), channel_id=1, source_target_pairs={{0,96},{16,112},{32,64},{48,80},{64,32},{80,48},{96,0},{112,16},{1... | collective-permute-start | bytes 110600 | tf_op jit(solution)/shard_map/step1/ppermute | solution.py:429
  106.9 0.6 collective-permute-start.17
  107.5 0.5 collective-permute-start.15
  108.0 2.7 %collective-permute-start.14 = (bf16[9,16,128]{2,1,0:T(8,128)(2,1)S(1)}, bf16[9,16,128]{2,1,0:T(8,128)(2,1)S(1)}, u32[]{:S(2)}, u32[]{:S(2)}) collective-permute-start(bf16[9,16,128]{2,1,0:T(8,128)(2,1)S(1)} %get-tuple-element.40.refs_2_), channel_id=1, source_target_pairs={{0,16},{16,0},{32,48},{48,32},{64,80},{80,64},{96,112},{112,96},{1... | collective-permute-start | bytes 110600 | tf_op jit(solution)/shard_map/step1/ppermute | solution.py:429
  110.7 1.5 collective-permute-start.20
  112.2 2.1 %collective-permute-start.18 = (bf16[9,16,128]{2,1,0:T(8,128)(2,1)S(1)}, bf16[9,16,128]{2,1,0:T(8,128)(2,1)S(1)}, u32[]{:S(2)}, u32[]{:S(2)}) collective-permute-start(bf16[9,16,128]{2,1,0:T(8,128)(2,1)S(1)} %collective-permute-done.17.refs_6_), channel_id=1, source_target_pairs={{0,16},{16,0},{32,48},{48,32},{64,80},{80,64},{96,112},{112,96},{1... | collective-permute-start | bytes 110600 | tf_op jit(solution)/shard_map/step1/ppermute | solution.py:429
  114.3 0.8 collective-permute-done.18.refs_7_
  115.5 7.2 %step1.2 = bf16[16,9,16,128]{3,2,1,0:T(8,128)(2,1)S(1)} custom-call(s32[1033]{0:T(1024)S(1)} %concatenate.6.row_idx.refs_2_, s32[1032]{0:T(1024)S(1)} %get-tuple-element.56.refs_4_.col_idx, bf16[129,256,256]{2,1,0:T(8,128)(2,1)S(1)} %get-tuple-element.34.refs_0_, bf16[129,256,256]{2,1,0:T(8,128)(2,1)S(1)} %get-tuple-element.35.refs_1_, ...), custom_call_target="tpu_custom_call" | custom-call | tf_op jit(solution)/shard_map/step1/pallas_call | solution.py:408
  122.6 14.4 %all_to_all.50.recv = bf16[16,9,16,128]{3,2,1,0:T(8,128)(2,1)S(1)} all-to-all(bf16[16,9,16,128]{3,2,1,0:T(8,128)(2,1)S(1)} %step1.2), channel_id=1, replica_groups=mesh['row'=8,'col'=16] {'col'}, dimensions={0} | all-to-all | bytes 1179648 | tf_op jit(solution)/shard_map/step1/all_to_all | solution.py:420
  137.1 1.5 step1.3
  138.6 0.9 collective-permute-start.26
  139.4 0.6 collective-permute-start.24
  140.0 1.9 collective-permute-start.22
  141.9 2.5 %collective-permute-start.21 = (bf16[9,16,128]{2,1,0:T(8,128)(2,1)S(1)}, bf16[9,16,128]{2,1,0:T(8,128)(2,1)S(1)}, u32[]{:S(2)}, u32[]{:S(2)}) collective-permute-start(bf16[9,16,128]{2,1,0:T(8,128)(2,1)S(1)} %get-tuple-element.44.refs_2_), channel_id=1, source_target_pairs={{0,16},{16,0},{32,48},{48,32},{64,80},{80,64},{96,112},{112,96},{1... | collective-permute-start | bytes 110600 | tf_op jit(solution)/shard_map/step2/ppermute | solution.py:429
  144.4 1.1 collective-permute-start.27
  145.5 1.3 collective-permute-start.25
  146.8 0.8 collective-permute-done.25.refs_7_
  148.0 7.2 %step2.2 = bf16[16,9,16,128]{3,2,1,0:T(8,128)(2,1)S(1)} custom-call(s32[1033]{0:T(1024)S(1)} %concatenate.6.row_idx.refs_2_, s32[1032]{0:T(1024)S(1)} %get-tuple-element.56.refs_4_.col_idx, bf16[129,256,256]{2,1,0:T(8,128)(2,1)S(1)} %get-tuple-element.34.refs_0_, bf16[129,256,256]{2,1,0:T(8,128)(2,1)S(1)} %get-tuple-element.35.refs_1_, ...), custom_call_target="tpu_custom_call" | custom-call | tf_op jit(solution)/shard_map/step2/pallas_call | solution.py:408
  155.2 14.4 %all_to_all.51.recv = bf16[16,9,16,128]{3,2,1,0:T(8,128)(2,1)S(1)} all-to-all(bf16[16,9,16,128]{3,2,1,0:T(8,128)(2,1)S(1)} %step2.2), channel_id=1, replica_groups=mesh['row'=8,'col'=16] {'col'}, dimensions={0} | all-to-all | bytes 1179648 | tf_op jit(solution)/shard_map/step2/all_to_all | solution.py:420
  169.6 1.5 step2.3
  171.1 16.2 %all_to_all.52 = bf16[128,4,128]{2,1,0:T(4,128)(2,1)S(1)} all-to-all(bf16[128,4,128]{2,1,0:T(4,128)(2,1)S(1)} %bitcast.11), channel_id=1, replica_groups=mesh['row'=8,'col'=16] {'row','col'}, dimensions={0} | all-to-all | bytes 262144 | tf_op jit(solution)/shard_map/finish/all_to_all | solution.py:420
  187.3 1.7 finish.1
  (36 shorter events, 2.9 us)
Async XLA Ops:
  25.7 19.9 %all-to-all-start.1 = ((bf16[128,32,128]{2,1,0:T(8,128)(2,1)}), bf16[128,32,128]{2,1,0:T(8,128)(2,1)S(1)}, u32[]{:S(2)}, u32[]{:S(2)}) async-start(bf16[128,32,128]{2,1,0:T(8,128)(2,1)} %get-tuple-element.30), calls=%async_computation.1 | async-start | bytes 2097152 | tf_op jit(solution)/shard_map/gather/all_to_all | solution.py:420
  30.3 4.8 %collective-permute-start.5 = (bf16[8,32,128]{2,1,0:T(8,128)(2,1)S(1)}, bf16[8,32,128]{2,1,0:T(8,128)(2,1)S(1)}, u32[]{:S(2)}, u32[]{:S(2)}) collective-permute-start(bf16[8,32,128]{2,1,0:T(8,128)(2,1)S(1)} %get-tuple-element.31.refs_0_), channel_id=1, source_target_pairs={{0,96},{16,112},{32,64},{48,80},{64,32},{80,48},{96,0},{112,16},{1... | collective-permute-start | bytes 196616 | tf_op jit(solution)/shard_map/gather/ppermute | solution.py:429
  30.9 6.0 %collective-permute-start.3 = (bf16[8,32,128]{2,1,0:T(8,128)(2,1)S(1)}, bf16[8,32,128]{2,1,0:T(8,128)(2,1)S(1)}, u32[]{:S(2)}, u32[]{:S(2)}) collective-permute-start(bf16[8,32,128]{2,1,0:T(8,128)(2,1)S(1)} %get-tuple-element.31.refs_0_), channel_id=1, source_target_pairs={{0,64},{16,80},{32,96},{48,112},{64,0},{80,16},{96,32},{112,48},{1... | collective-permute-start | bytes 196616 | tf_op jit(solution)/shard_map/gather/ppermute | solution.py:429
  32.6 5.0 %collective-permute-start.1 = (bf16[8,32,128]{2,1,0:T(8,128)(2,1)S(1)}, bf16[8,32,128]{2,1,0:T(8,128)(2,1)S(1)}, u32[]{:S(2)}, u32[]{:S(2)}) collective-permute-start(bf16[8,32,128]{2,1,0:T(8,128)(2,1)S(1)} %get-tuple-element.31.refs_0_), channel_id=1, source_target_pairs={{0,32},{16,48},{32,0},{48,16},{64,96},{80,112},{96,64},{112,80},{1... | collective-permute-start | bytes 196616 | tf_op jit(solution)/shard_map/gather/ppermute | solution.py:429
  33.5 4.6 %collective-permute-start = (bf16[8,32,128]{2,1,0:T(8,128)(2,1)S(1)}, bf16[8,32,128]{2,1,0:T(8,128)(2,1)S(1)}, u32[]{:S(2)}, u32[]{:S(2)}) collective-permute-start(bf16[8,32,128]{2,1,0:T(8,128)(2,1)S(1)} %get-tuple-element.31.refs_0_), channel_id=1, source_target_pairs={{0,16},{16,0},{32,48},{48,32},{64,80},{80,64},{96,112},{112,96},{1... | collective-permute-start | bytes 196616 | tf_op jit(solution)/shard_map/gather/ppermute | solution.py:429
  35.1 3.1 %collective-permute-start.6 = (bf16[8,32,128]{2,1,0:T(8,128)(2,1)S(1)}, bf16[8,32,128]{2,1,0:T(8,128)(2,1)S(1)}, u32[]{:S(2)}, u32[]{:S(2)}) collective-permute-start(bf16[8,32,128]{2,1,0:T(8,128)(2,1)S(1)} %collective-permute-done.5.refs_6_), channel_id=1, source_target_pairs={{0,16},{16,0},{32,48},{48,32},{64,80},{80,64},{96,112},{112,96},{1... | collective-permute-start | bytes 196616 | tf_op jit(solution)/shard_map/gather/ppermute | solution.py:429
  36.9 1.6 collective-permute-start.4
  37.7 1.4 collective-permute-start.2
  45.6 26.3 %copy-start = (f32[16,8,128]{2,1,0:T(8,128)S(1)}, f32[16,8,128]{2,1,0:T(8,128)}, u32[]{:S(2)}) copy-start(f32[16,8,128]{2,1,0:T(8,128)} %start_ref.1) | copy-start | bytes 196612
  72.3 6.0 %collective-permute-start.12 = (bf16[9,16,128]{2,1,0:T(8,128)(2,1)S(1)}, bf16[9,16,128]{2,1,0:T(8,128)(2,1)S(1)}, u32[]{:S(2)}, u32[]{:S(2)}) collective-permute-start(bf16[9,16,128]{2,1,0:T(8,128)(2,1)S(1)} %get-tuple-element.37.refs_2_), channel_id=1, source_target_pairs={{0,96},{16,112},{32,64},{48,80},{64,32},{80,48},{96,0},{112,16},{1... | collective-permute-start | bytes 110600 | tf_op jit(solution)/shard_map/step0/ppermute | solution.py:429
  72.9 6.5 %collective-permute-start.10 = (bf16[9,16,128]{2,1,0:T(8,128)(2,1)S(1)}, bf16[9,16,128]{2,1,0:T(8,128)(2,1)S(1)}, u32[]{:S(2)}, u32[]{:S(2)}) collective-permute-start(bf16[9,16,128]{2,1,0:T(8,128)(2,1)S(1)} %get-tuple-element.37.refs_2_), channel_id=1, source_target_pairs={{0,64},{16,80},{32,96},{48,112},{64,0},{80,16},{96,32},{112,48},{1... | collective-permute-start | bytes 110600 | tf_op jit(solution)/shard_map/step0/ppermute | solution.py:429
  74.7 5.9 %collective-permute-start.8 = (bf16[9,16,128]{2,1,0:T(8,128)(2,1)S(1)}, bf16[9,16,128]{2,1,0:T(8,128)(2,1)S(1)}, u32[]{:S(2)}, u32[]{:S(2)}) collective-permute-start(bf16[9,16,128]{2,1,0:T(8,128)(2,1)S(1)} %get-tuple-element.37.refs_2_), channel_id=1, source_target_pairs={{0,32},{16,48},{32,0},{48,16},{64,96},{80,112},{96,64},{112,80},{1... | collective-permute-start | bytes 110600 | tf_op jit(solution)/shard_map/step0/ppermute | solution.py:429
  75.5 5.5 %collective-permute-start.7 = (bf16[9,16,128]{2,1,0:T(8,128)(2,1)S(1)}, bf16[9,16,128]{2,1,0:T(8,128)(2,1)S(1)}, u32[]{:S(2)}, u32[]{:S(2)}) collective-permute-start(bf16[9,16,128]{2,1,0:T(8,128)(2,1)S(1)} %get-tuple-element.37.refs_2_), channel_id=1, source_target_pairs={{0,16},{16,0},{32,48},{48,32},{64,80},{80,64},{96,112},{112,96},{1... | collective-permute-start | bytes 110600 | tf_op jit(solution)/shard_map/step0/ppermute | solution.py:429
  78.3 2.8 %collective-permute-start.13 = (bf16[9,16,128]{2,1,0:T(8,128)(2,1)S(1)}, bf16[9,16,128]{2,1,0:T(8,128)(2,1)S(1)}, u32[]{:S(2)}, u32[]{:S(2)}) collective-permute-start(bf16[9,16,128]{2,1,0:T(8,128)(2,1)S(1)} %collective-permute-done.12.refs_8_), channel_id=1, source_target_pairs={{0,16},{16,0},{32,48},{48,32},{64,80},{80,64},{96,112},{112,96},{1... | collective-permute-start | bytes 110600 | tf_op jit(solution)/shard_map/step0/ppermute | solution.py:429
  79.4 2.1 %collective-permute-start.11 = (bf16[9,16,128]{2,1,0:T(8,128)(2,1)S(1)}, bf16[9,16,128]{2,1,0:T(8,128)(2,1)S(1)}, u32[]{:S(2)}, u32[]{:S(2)}) collective-permute-start(bf16[9,16,128]{2,1,0:T(8,128)(2,1)S(1)} %collective-permute-done.10.refs_6_), channel_id=1, source_target_pairs={{0,16},{16,0},{32,48},{48,32},{64,80},{80,64},{96,112},{112,96},{1... | collective-permute-start | bytes 110600 | tf_op jit(solution)/shard_map/step0/ppermute | solution.py:429
  80.6 1.3 collective-permute-start.9
  104.7 6.0 %collective-permute-start.19 = (bf16[9,16,128]{2,1,0:T(8,128)(2,1)S(1)}, bf16[9,16,128]{2,1,0:T(8,128)(2,1)S(1)}, u32[]{:S(2)}, u32[]{:S(2)}) collective-permute-start(bf16[9,16,128]{2,1,0:T(8,128)(2,1)S(1)} %get-tuple-element.40.refs_2_), channel_id=1, source_target_pairs={{0,96},{16,112},{32,64},{48,80},{64,32},{80,48},{96,0},{112,16},{1... | collective-permute-start | bytes 110600 | tf_op jit(solution)/shard_map/step1/ppermute | solution.py:429
  106.9 5.2 %collective-permute-start.17 = (bf16[9,16,128]{2,1,0:T(8,128)(2,1)S(1)}, bf16[9,16,128]{2,1,0:T(8,128)(2,1)S(1)}, u32[]{:S(2)}, u32[]{:S(2)}) collective-permute-start(bf16[9,16,128]{2,1,0:T(8,128)(2,1)S(1)} %get-tuple-element.40.refs_2_), channel_id=1, source_target_pairs={{0,64},{16,80},{32,96},{48,112},{64,0},{80,16},{96,32},{112,48},{1... | collective-permute-start | bytes 110600 | tf_op jit(solution)/shard_map/step1/ppermute | solution.py:429
  107.5 6.7 %collective-permute-start.15 = (bf16[9,16,128]{2,1,0:T(8,128)(2,1)S(1)}, bf16[9,16,128]{2,1,0:T(8,128)(2,1)S(1)}, u32[]{:S(2)}, u32[]{:S(2)}) collective-permute-start(bf16[9,16,128]{2,1,0:T(8,128)(2,1)S(1)} %get-tuple-element.40.refs_2_), channel_id=1, source_target_pairs={{0,32},{16,48},{32,0},{48,16},{64,96},{80,112},{96,64},{112,80},{1... | collective-permute-start | bytes 110600 | tf_op jit(solution)/shard_map/step1/ppermute | solution.py:429
  108.0 6.3 %collective-permute-start.14 = (bf16[9,16,128]{2,1,0:T(8,128)(2,1)S(1)}, bf16[9,16,128]{2,1,0:T(8,128)(2,1)S(1)}, u32[]{:S(2)}, u32[]{:S(2)}) collective-permute-start(bf16[9,16,128]{2,1,0:T(8,128)(2,1)S(1)} %get-tuple-element.40.refs_2_), channel_id=1, source_target_pairs={{0,16},{16,0},{32,48},{48,32},{64,80},{80,64},{96,112},{112,96},{1... | collective-permute-start | bytes 110600 | tf_op jit(solution)/shard_map/step1/ppermute | solution.py:429
  110.7 3.6 %collective-permute-start.20 = (bf16[9,16,128]{2,1,0:T(8,128)(2,1)S(1)}, bf16[9,16,128]{2,1,0:T(8,128)(2,1)S(1)}, u32[]{:S(2)}, u32[]{:S(2)}) collective-permute-start(bf16[9,16,128]{2,1,0:T(8,128)(2,1)S(1)} %collective-permute-done.19.refs_8_), channel_id=1, source_target_pairs={{0,16},{16,0},{32,48},{48,32},{64,80},{80,64},{96,112},{112,96},{1... | collective-permute-start | bytes 110600 | tf_op jit(solution)/shard_map/step1/ppermute | solution.py:429
  112.2 3.0 %collective-permute-start.18 = (bf16[9,16,128]{2,1,0:T(8,128)(2,1)S(1)}, bf16[9,16,128]{2,1,0:T(8,128)(2,1)S(1)}, u32[]{:S(2)}, u32[]{:S(2)}) collective-permute-start(bf16[9,16,128]{2,1,0:T(8,128)(2,1)S(1)} %collective-permute-done.17.refs_6_), channel_id=1, source_target_pairs={{0,16},{16,0},{32,48},{48,32},{64,80},{80,64},{96,112},{112,96},{1... | collective-permute-start | bytes 110600 | tf_op jit(solution)/shard_map/step1/ppermute | solution.py:429
  114.3 1.2 collective-permute-start.16
  138.6 5.8 %collective-permute-start.26 = (bf16[9,16,128]{2,1,0:T(8,128)(2,1)S(1)}, bf16[9,16,128]{2,1,0:T(8,128)(2,1)S(1)}, u32[]{:S(2)}, u32[]{:S(2)}) collective-permute-start(bf16[9,16,128]{2,1,0:T(8,128)(2,1)S(1)} %get-tuple-element.44.refs_2_), channel_id=1, source_target_pairs={{0,96},{16,112},{32,64},{48,80},{64,32},{80,48},{96,0},{112,16},{1... | collective-permute-start | bytes 110600 | tf_op jit(solution)/shard_map/step2/ppermute | solution.py:429
  139.4 6.0 %collective-permute-start.24 = (bf16[9,16,128]{2,1,0:T(8,128)(2,1)S(1)}, bf16[9,16,128]{2,1,0:T(8,128)(2,1)S(1)}, u32[]{:S(2)}, u32[]{:S(2)}) collective-permute-start(bf16[9,16,128]{2,1,0:T(8,128)(2,1)S(1)} %get-tuple-element.44.refs_2_), channel_id=1, source_target_pairs={{0,64},{16,80},{32,96},{48,112},{64,0},{80,16},{96,32},{112,48},{1... | collective-permute-start | bytes 110600 | tf_op jit(solution)/shard_map/step2/ppermute | solution.py:429
  140.0 6.7 %collective-permute-start.22 = (bf16[9,16,128]{2,1,0:T(8,128)(2,1)S(1)}, bf16[9,16,128]{2,1,0:T(8,128)(2,1)S(1)}, u32[]{:S(2)}, u32[]{:S(2)}) collective-permute-start(bf16[9,16,128]{2,1,0:T(8,128)(2,1)S(1)} %get-tuple-element.44.refs_2_), channel_id=1, source_target_pairs={{0,32},{16,48},{32,0},{48,16},{64,96},{80,112},{96,64},{112,80},{1... | collective-permute-start | bytes 110600 | tf_op jit(solution)/shard_map/step2/ppermute | solution.py:429
  141.9 4.9 %collective-permute-start.21 = (bf16[9,16,128]{2,1,0:T(8,128)(2,1)S(1)}, bf16[9,16,128]{2,1,0:T(8,128)(2,1)S(1)}, u32[]{:S(2)}, u32[]{:S(2)}) collective-permute-start(bf16[9,16,128]{2,1,0:T(8,128)(2,1)S(1)} %get-tuple-element.44.refs_2_), channel_id=1, source_target_pairs={{0,16},{16,0},{32,48},{48,32},{64,80},{80,64},{96,112},{112,96},{1... | collective-permute-start | bytes 110600 | tf_op jit(solution)/shard_map/step2/ppermute | solution.py:429
  144.4 2.4 %collective-permute-start.27 = (bf16[9,16,128]{2,1,0:T(8,128)(2,1)S(1)}, bf16[9,16,128]{2,1,0:T(8,128)(2,1)S(1)}, u32[]{:S(2)}, u32[]{:S(2)}) collective-permute-start(bf16[9,16,128]{2,1,0:T(8,128)(2,1)S(1)} %collective-permute-done.26.refs_8_), channel_id=1, source_target_pairs={{0,16},{16,0},{32,48},{48,32},{64,80},{80,64},{96,112},{112,96},{1... | collective-permute-start | bytes 110600 | tf_op jit(solution)/shard_map/step2/ppermute | solution.py:429
  145.5 2.2 %collective-permute-start.25 = (bf16[9,16,128]{2,1,0:T(8,128)(2,1)S(1)}, bf16[9,16,128]{2,1,0:T(8,128)(2,1)S(1)}, u32[]{:S(2)}, u32[]{:S(2)}) collective-permute-start(bf16[9,16,128]{2,1,0:T(8,128)(2,1)S(1)} %collective-permute-done.24.refs_6_), channel_id=1, source_target_pairs={{0,16},{16,0},{32,48},{48,32},{64,80},{80,64},{96,112},{112,96},{1... | collective-permute-start | bytes 110600 | tf_op jit(solution)/shard_map/step2/ppermute | solution.py:429
  146.8 1.2 collective-permute-start.23
where the time goes:
time: 189 us
  blocking collectives  91.5 us (48%)
  Pallas kernels  48.3 us (26%)
  starting transfers between devices  38.1 us (20%)
  waiting for transfers between devices  9.41 us (5%)
    all_to_all x6, blocking collectives, exchange(): return lax.all_to_all(values, axis, split_axis=0, concat_axis=0, tiled=True)  91.5 us
    pallas_call x13, Pallas kernels, call(): pl.pallas_call(kernel, out_shape=out_shape, in_specs=specs or [whole()] *...  48.3 us
    ppermute x28, starting transfers between devices, toggled(): return lax.ppermute(values, 'row', [(i, i ^ bits) for i in range(size)])  34.4 us
    all_to_all x1, waiting for transfers between devices, exchange(): return lax.all_to_all(values, axis, split_axis=0, concat_axis=0, tiled=True)  5.24 us
    ppermute x28, waiting for transfers between devices, toggled(): return lax.ppermute(values, 'row', [(i, i ^ bits) for i in range(size)])  4.17 us
  transfers between devices with their start and end apart: 29, of which 9 were waited for; matrix products, arithmetic and copies ran while one was open for 0% of the time, Pallas kernels for 1%

commit v1 on v0

--- a/solution.py
+++ b/solution.py
@@ -144,18 +144,16 @@
 
 def features(block, sign):
     values = block.astype(F32)
-    pieces = split3(jnp.sum(values * values, axis=0, keepdims=True))
-    rows = iota((BLOCK - FEAT, BLOCK), 0)
-    tail = jnp.zeros((BLOCK - FEAT, BLOCK), F32)
+    pieces = split3(jnp.sum(values * values, axis=0, keepdims=True) * EXP2_SCALE)
+    height = BLOCK - 3 * FEAT
+    rows = iota((height, BLOCK), 0)
+    tail = jnp.zeros((height, BLOCK), F32)
     for n in range(3):
-        if sign:
-            tail = jnp.where(rows == n, -pieces[n], tail)
-            tail = jnp.where(rows == n + 3, 1.0, tail)
-        else:
-            tail = jnp.where(rows == n, 1.0, tail)
-            tail = jnp.where(rows == n + 3, -pieces[n], tail)
-    scale = 2.0 if sign else 1.0
-    return jnp.concatenate([values * scale, tail], axis=0).astype(BF16)
+        square, one = (n, n + 3) if sign else (n + 3, n)
+        tail = jnp.where(rows == square, -pieces[n], tail)
+        tail = jnp.where(rows == one, 1.0, tail)
+    main = split3(values * (2.0 * EXP2_SCALE)) if sign else (values,) * 3
+    return jnp.concatenate([*main, tail], axis=0).astype(BF16)
 
 
 def each_piece(pieces, body, unroll):
@@ -204,7 +202,7 @@
                 i = row_idx[(first + group) * 4 + q]
                 j = col_idx[(first + group) * 4 + q]
                 power = jnp.dot(left[j], right[i], preferred_element_type=F32)
-                block = jnp.exp2(power * EXP2_SCALE).astype(BF16)
+                block = jnp.exp2(power).astype(BF16)
                 r, c = q // 2, q % 2
                 weights[group, r * BLOCK : (r + 1) * BLOCK, c * BLOCK : (c + 1) * BLOCK] = block
                 total[i] += jnp.sum(block.astype(F32).reshape(BLOCK // 8, 8, BLOCK), axis=0)

time: 189 us -> 188 us (level)
  no operation moved by 1% of the time
where the time goes in v1:
time: 188 us
  blocking collectives  91.5 us (49%)
  Pallas kernels  47.8 us (25%)
  starting transfers between devices  38.1 us (20%)
  waiting for transfers between devices  8.7 us (5%)
    all_to_all x6, blocking collectives, exchange(): return lax.all_to_all(values, axis, split_axis=0, concat_axis=0, tiled=True)  91.5 us
    pallas_call x13, Pallas kernels, call(): pl.pallas_call(kernel, out_shape=out_shape, in_specs=specs or [whole()] *...  47.8 us
    ppermute x28, starting transfers between devices, toggled(): return lax.ppermute(values, 'row', [(i, i ^ bits) for i in range(size)])  34.4 us
    all_to_all x1, waiting for transfers between devices, exchange(): return lax.all_to_all(values, axis, split_axis=0, concat_axis=0, tiled=True)  4.54 us
    ppermute x28, waiting for transfers between devices, toggled(): return lax.ppermute(values, 'row', [(i, i ^ bits) for i in range(size)])  4.17 us
  transfers between devices with their start and end apart: 29, of which 9 were waited for; matrix products, arithmetic and copies ran while one was open for 0% of the time, Pallas kernels for 1%

profile of v1, /device:TPU:1, one launch (start us, length us, event | category | flops | bytes accessed | tf_op | source)
XLA Modules:
  0.0 187.8 jit_solution(12167684916880527661)
XLA Ops:
  0.6 2.0 %relay.2 = (bf16[512,128]{1,0:T(8,128)(2,1)S(1)}, s32[8,128]{1,0:T(8,128)S(1)}) custom-call(s32[16,128]{1,0:T(8,128)} %bitcast.15, bf16[32,2048]{1,0:T(8,128)(2,1)} %desc_in.1, s32[8,128]{1,0:T(8,128)} %bitcast.16), custom_call_target="tpu_custom_call" | custom-call | tf_op jit(solution)/shard_map/relay/pallas_call | solution.py:406
  2.7 21.5 %all_to_all.47 = bf16[128,4,128]{2,1,0:T(4,128)(2,1)S(1)} all-to-all(bf16[128,4,128]{2,1,0:T(4,128)(2,1)S(1)} %bitcast.12), channel_id=1, replica_groups=mesh['row'=8,'col'=16] {'row','col'}, dimensions={0} | all-to-all | bytes 262144 | tf_op jit(solution)/shard_map/relay/all_to_all | solution.py:418
  24.2 1.5 relay.3
  25.7 3.7 %all-to-all-start.1 = ((bf16[128,32,128]{2,1,0:T(8,128)(2,1)}), bf16[128,32,128]{2,1,0:T(8,128)(2,1)S(1)}, u32[]{:S(2)}, u32[]{:S(2)}) async-start(bf16[128,32,128]{2,1,0:T(8,128)(2,1)} %get-tuple-element.30), calls=%async_computation.1 | async-start | bytes 2097152 | tf_op jit(solution)/shard_map/gather/all_to_all | solution.py:418
  29.4 0.8 fusion.3
  30.3 0.6 collective-permute-start.5
  30.9 1.7 collective-permute-start.3
  32.6 0.9 collective-permute-start.1
  33.5 1.5 collective-permute-start
  35.1 1.8 collective-permute-start.6
  36.9 0.7 collective-permute-start.4
  38.6 0.5 collective-permute-done.2.refs_3_
  39.1 2.0 %gather.1.refs_1_.left = bf16[64,128,128]{2,1,0:T(8,128)(2,1)S(1)} custom-call(s32[1033]{0:T(1024)S(1)} %concatenate.6.row_idx.refs_2_, bf16[8,32,128]{2,1,0:T(8,128)(2,1)S(1)} %get-tuple-element.31.refs_0_, bf16[8,32,128]{2,1,0:T(8,128)(2,1)S(1)} %collective-permute-done.refs_1_, bf16[8,32,128]{2,1,0:T(8,128)(2,1)S(1)} %collective-permute-done.1.refs_2_, ...), custom_call_target="tpu_custom_call" | custom-call | tf_op jit(solution)/shard_map/gather/pallas_call | solution.py:406
  41.1 4.5 %all-to-all-done.1.refs_0_.row_desc = bf16[128,32,128]{2,1,0:T(8,128)(2,1)S(1)} async-done(((bf16[128,32,128]{2,1,0:T(8,128)(2,1)}), bf16[128,32,128]{2,1,0:T(8,128)(2,1)S(1)}, u32[]{:S(2)}, u32[]{:S(2)}) %all-to-all-start.1) | async-done | bytes 1048608 | tf_op jit(solution)/shard_map/gather/all_to_all | solution.py:418
  45.6 14.3 %build.3 = (bf16[129,256,256]{2,1,0:T(8,128)(2,1)S(1)}, bf16[129,256,256]{2,1,0:T(8,128)(2,1)S(1)}, f32[16,8,128]{2,1,0:T(8,128)S(1)}) custom-call(s32[1033]{0:T(1024)S(1)} %concatenate.6.row_idx.refs_2_, s32[1032]{0:T(1024)S(1)} %get-tuple-element.55.refs_3_.col_idx, ...), custom_call_target="tpu_custom_call", output_to_operand_aliasing={{0}: (4, {}), {1}: (5, {})} | custom-call | tf_op jit(solution)/shard_map/build/pallas_call | solution.py:406
  60.0 10.8 %all_to_all.48.degree_ref = f32[16,8,128]{2,1,0:T(8,128)S(1)} all-to-all(f32[16,8,128]{2,1,0:T(8,128)S(1)} %get-tuple-element.36), channel_id=1, replica_groups=mesh['row'=8,'col'=16] {'col'}, dimensions={0} | all-to-all | bytes 131072 | tf_op jit(solution)/shard_map/degree/all_to_all | solution.py:418
  71.1 0.6 collective-permute-start.12
  71.7 1.7 collective-permute-start.10
  73.5 0.9 collective-permute-start.8
  74.4 2.8 %collective-permute-start.7 = (bf16[9,16,128]{2,1,0:T(8,128)(2,1)S(1)}, bf16[9,16,128]{2,1,0:T(8,128)(2,1)S(1)}, u32[]{:S(2)}, u32[]{:S(2)}) collective-permute-start(bf16[9,16,128]{2,1,0:T(8,128)(2,1)S(1)} %get-tuple-element.37.refs_2_), channel_id=1, source_target_pairs={{0,16},{16,0},{32,48},{48,32},{64,80},{80,64},{96,112},{112,96},{1... | collective-permute-start | bytes 110600 | tf_op jit(solution)/shard_map/step0/ppermute | solution.py:427
  77.1 1.1 collective-permute-start.13
  78.2 1.2 collective-permute-start.11
  79.4 0.5 collective-permute-start.9
  80.3 0.5 collective-permute-done.9.refs_5_
  80.8 7.2 %step0.2 = bf16[16,9,16,128]{3,2,1,0:T(8,128)(2,1)S(1)} custom-call(s32[1033]{0:T(1024)S(1)} %concatenate.6.row_idx.refs_2_, s32[1032]{0:T(1024)S(1)} %get-tuple-element.56.refs_4_.col_idx, bf16[129,256,256]{2,1,0:T(8,128)(2,1)S(1)} %get-tuple-element.34.refs_0_, bf16[129,256,256]{2,1,0:T(8,128)(2,1)S(1)} %get-tuple-element.35.refs_1_, ...), custom_call_target="tpu_custom_call" | custom-call | tf_op jit(solution)/shard_map/step0/pallas_call | solution.py:406
  88.0 14.3 %all_to_all.49.recv = bf16[16,9,16,128]{3,2,1,0:T(8,128)(2,1)S(1)} all-to-all(bf16[16,9,16,128]{3,2,1,0:T(8,128)(2,1)S(1)} %step0.2), channel_id=1, replica_groups=mesh['row'=8,'col'=16] {'col'}, dimensions={0} | all-to-all | bytes 1179648 | tf_op jit(solution)/shard_map/step0/all_to_all | solution.py:418
  102.2 1.4 step0.3
  103.6 2.2 %collective-permute-start.19 = (bf16[9,16,128]{2,1,0:T(8,128)(2,1)S(1)}, bf16[9,16,128]{2,1,0:T(8,128)(2,1)S(1)}, u32[]{:S(2)}, u32[]{:S(2)}) collective-permute-start(bf16[9,16,128]{2,1,0:T(8,128)(2,1)S(1)} %get-tuple-element.40.refs_2_), channel_id=1, source_target_pairs={{0,96},{16,112},{32,64},{48,80},{64,32},{80,48},{96,0},{112,16},{1... | collective-permute-start | bytes 110600 | tf_op jit(solution)/shard_map/step1/ppermute | solution.py:427
  105.7 0.7 collective-permute-start.17
  106.9 2.6 %collective-permute-start.14 = (bf16[9,16,128]{2,1,0:T(8,128)(2,1)S(1)}, bf16[9,16,128]{2,1,0:T(8,128)(2,1)S(1)}, u32[]{:S(2)}, u32[]{:S(2)}) collective-permute-start(bf16[9,16,128]{2,1,0:T(8,128)(2,1)S(1)} %get-tuple-element.40.refs_2_), channel_id=1, source_target_pairs={{0,16},{16,0},{32,48},{48,32},{64,80},{80,64},{96,112},{112,96},{1... | collective-permute-start | bytes 110600 | tf_op jit(solution)/shard_map/step1/ppermute | solution.py:427
  109.5 1.5 collective-permute-start.20
  111.0 2.1 %collective-permute-start.18 = (bf16[9,16,128]{2,1,0:T(8,128)(2,1)S(1)}, bf16[9,16,128]{2,1,0:T(8,128)(2,1)S(1)}, u32[]{:S(2)}, u32[]{:S(2)}) collective-permute-start(bf16[9,16,128]{2,1,0:T(8,128)(2,1)S(1)} %collective-permute-done.17.refs_6_), channel_id=1, source_target_pairs={{0,16},{16,0},{32,48},{48,32},{64,80},{80,64},{96,112},{112,96},{1... | collective-permute-start | bytes 110600 | tf_op jit(solution)/shard_map/step1/ppermute | solution.py:427
  113.1 0.8 collective-permute-done.18.refs_7_
  114.3 7.2 %step1.2 = bf16[16,9,16,128]{3,2,1,0:T(8,128)(2,1)S(1)} custom-call(s32[1033]{0:T(1024)S(1)} %concatenate.6.row_idx.refs_2_, s32[1032]{0:T(1024)S(1)} %get-tuple-element.56.refs_4_.col_idx, bf16[129,256,256]{2,1,0:T(8,128)(2,1)S(1)} %get-tuple-element.34.refs_0_, bf16[129,256,256]{2,1,0:T(8,128)(2,1)S(1)} %get-tuple-element.35.refs_1_, ...), custom_call_target="tpu_custom_call" | custom-call | tf_op jit(solution)/shard_map/step1/pallas_call | solution.py:406
  121.5 14.4 %all_to_all.50.recv = bf16[16,9,16,128]{3,2,1,0:T(8,128)(2,1)S(1)} all-to-all(bf16[16,9,16,128]{3,2,1,0:T(8,128)(2,1)S(1)} %step1.2), channel_id=1, replica_groups=mesh['row'=8,'col'=16] {'col'}, dimensions={0} | all-to-all | bytes 1179648 | tf_op jit(solution)/shard_map/step1/all_to_all | solution.py:418
  135.9 1.5 step1.3
  137.4 0.9 collective-permute-start.26
  138.3 0.7 collective-permute-start.24
  139.0 1.8 collective-permute-start.22
  140.7 2.5 %collective-permute-start.21 = (bf16[9,16,128]{2,1,0:T(8,128)(2,1)S(1)}, bf16[9,16,128]{2,1,0:T(8,128)(2,1)S(1)}, u32[]{:S(2)}, u32[]{:S(2)}) collective-permute-start(bf16[9,16,128]{2,1,0:T(8,128)(2,1)S(1)} %get-tuple-element.44.refs_2_), channel_id=1, source_target_pairs={{0,16},{16,0},{32,48},{48,32},{64,80},{80,64},{96,112},{112,96},{1... | collective-permute-start | bytes 110600 | tf_op jit(solution)/shard_map/step2/ppermute | solution.py:427
  143.2 1.1 collective-permute-start.27
  144.3 1.4 collective-permute-start.25
  145.7 0.8 collective-permute-done.25.refs_7_
  146.9 7.2 %step2.2 = bf16[16,9,16,128]{3,2,1,0:T(8,128)(2,1)S(1)} custom-call(s32[1033]{0:T(1024)S(1)} %concatenate.6.row_idx.refs_2_, s32[1032]{0:T(1024)S(1)} %get-tuple-element.56.refs_4_.col_idx, bf16[129,256,256]{2,1,0:T(8,128)(2,1)S(1)} %get-tuple-element.34.refs_0_, bf16[129,256,256]{2,1,0:T(8,128)(2,1)S(1)} %get-tuple-element.35.refs_1_, ...), custom_call_target="tpu_custom_call" | custom-call | tf_op jit(solution)/shard_map/step2/pallas_call | solution.py:406
  154.0 14.4 %all_to_all.51.recv = bf16[16,9,16,128]{3,2,1,0:T(8,128)(2,1)S(1)} all-to-all(bf16[16,9,16,128]{3,2,1,0:T(8,128)(2,1)S(1)} %step2.2), channel_id=1, replica_groups=mesh['row'=8,'col'=16] {'col'}, dimensions={0} | all-to-all | bytes 1179648 | tf_op jit(solution)/shard_map/step2/all_to_all | solution.py:418
  168.4 1.5 step2.3
  170.0 16.1 %all_to_all.52 = bf16[128,4,128]{2,1,0:T(4,128)(2,1)S(1)} all-to-all(bf16[128,4,128]{2,1,0:T(4,128)(2,1)S(1)} %bitcast.11), channel_id=1, replica_groups=mesh['row'=8,'col'=16] {'row','col'}, dimensions={0} | all-to-all | bytes 262144 | tf_op jit(solution)/shard_map/finish/all_to_all | solution.py:418
  186.1 1.7 finish.1
  (36 shorter events, 2.9 us)
Async XLA Ops:
  25.7 19.9 %all-to-all-start.1 = ((bf16[128,32,128]{2,1,0:T(8,128)(2,1)}), bf16[128,32,128]{2,1,0:T(8,128)(2,1)S(1)}, u32[]{:S(2)}, u32[]{:S(2)}) async-start(bf16[128,32,128]{2,1,0:T(8,128)(2,1)} %get-tuple-element.30), calls=%async_computation.1 | async-start | bytes 2097152 | tf_op jit(solution)/shard_map/gather/all_to_all | solution.py:418
  30.3 4.8 %collective-permute-start.5 = (bf16[8,32,128]{2,1,0:T(8,128)(2,1)S(1)}, bf16[8,32,128]{2,1,0:T(8,128)(2,1)S(1)}, u32[]{:S(2)}, u32[]{:S(2)}) collective-permute-start(bf16[8,32,128]{2,1,0:T(8,128)(2,1)S(1)} %get-tuple-element.31.refs_0_), channel_id=1, source_target_pairs={{0,96},{16,112},{32,64},{48,80},{64,32},{80,48},{96,0},{112,16},{1... | collective-permute-start | bytes 196616 | tf_op jit(solution)/shard_map/gather/ppermute | solution.py:427
  30.9 6.0 %collective-permute-start.3 = (bf16[8,32,128]{2,1,0:T(8,128)(2,1)S(1)}, bf16[8,32,128]{2,1,0:T(8,128)(2,1)S(1)}, u32[]{:S(2)}, u32[]{:S(2)}) collective-permute-start(bf16[8,32,128]{2,1,0:T(8,128)(2,1)S(1)} %get-tuple-element.31.refs_0_), channel_id=1, source_target_pairs={{0,64},{16,80},{32,96},{48,112},{64,0},{80,16},{96,32},{112,48},{1... | collective-permute-start | bytes 196616 | tf_op jit(solution)/shard_map/gather/ppermute | solution.py:427
  32.6 5.0 %collective-permute-start.1 = (bf16[8,32,128]{2,1,0:T(8,128)(2,1)S(1)}, bf16[8,32,128]{2,1,0:T(8,128)(2,1)S(1)}, u32[]{:S(2)}, u32[]{:S(2)}) collective-permute-start(bf16[8,32,128]{2,1,0:T(8,128)(2,1)S(1)} %get-tuple-element.31.refs_0_), channel_id=1, source_target_pairs={{0,32},{16,48},{32,0},{48,16},{64,96},{80,112},{96,64},{112,80},{1... | collective-permute-start | bytes 196616 | tf_op jit(solution)/shard_map/gather/ppermute | solution.py:427
  33.5 4.6 %collective-permute-start = (bf16[8,32,128]{2,1,0:T(8,128)(2,1)S(1)}, bf16[8,32,128]{2,1,0:T(8,128)(2,1)S(1)}, u32[]{:S(2)}, u32[]{:S(2)}) collective-permute-start(bf16[8,32,128]{2,1,0:T(8,128)(2,1)S(1)} %get-tuple-element.31.refs_0_), channel_id=1, source_target_pairs={{0,16},{16,0},{32,48},{48,32},{64,80},{80,64},{96,112},{112,96},{1... | collective-permute-start | bytes 196616 | tf_op jit(solution)/shard_map/gather/ppermute | solution.py:427
  35.1 3.1 %collective-permute-start.6 = (bf16[8,32,128]{2,1,0:T(8,128)(2,1)S(1)}, bf16[8,32,128]{2,1,0:T(8,128)(2,1)S(1)}, u32[]{:S(2)}, u32[]{:S(2)}) collective-permute-start(bf16[8,32,128]{2,1,0:T(8,128)(2,1)S(1)} %collective-permute-done.5.refs_6_), channel_id=1, source_target_pairs={{0,16},{16,0},{32,48},{48,32},{64,80},{80,64},{96,112},{112,96},{1... | collective-permute-start | bytes 196616 | tf_op jit(solution)/shard_map/gather/ppermute | solution.py:427
  36.9 1.6 collective-permute-start.4
  37.7 1.4 collective-permute-start.2
  45.6 25.1 %copy-start = (f32[16,8,128]{2,1,0:T(8,128)S(1)}, f32[16,8,128]{2,1,0:T(8,128)}, u32[]{:S(2)}) copy-start(f32[16,8,128]{2,1,0:T(8,128)} %start_ref.1) | copy-start | bytes 196612
  71.1 6.0 %collective-permute-start.12 = (bf16[9,16,128]{2,1,0:T(8,128)(2,1)S(1)}, bf16[9,16,128]{2,1,0:T(8,128)(2,1)S(1)}, u32[]{:S(2)}, u32[]{:S(2)}) collective-permute-start(bf16[9,16,128]{2,1,0:T(8,128)(2,1)S(1)} %get-tuple-element.37.refs_2_), channel_id=1, source_target_pairs={{0,96},{16,112},{32,64},{48,80},{64,32},{80,48},{96,0},{112,16},{1... | collective-permute-start | bytes 110600 | tf_op jit(solution)/shard_map/step0/ppermute | solution.py:427
  71.7 6.5 %collective-permute-start.10 = (bf16[9,16,128]{2,1,0:T(8,128)(2,1)S(1)}, bf16[9,16,128]{2,1,0:T(8,128)(2,1)S(1)}, u32[]{:S(2)}, u32[]{:S(2)}) collective-permute-start(bf16[9,16,128]{2,1,0:T(8,128)(2,1)S(1)} %get-tuple-element.37.refs_2_), channel_id=1, source_target_pairs={{0,64},{16,80},{32,96},{48,112},{64,0},{80,16},{96,32},{112,48},{1... | collective-permute-start | bytes 110600 | tf_op jit(solution)/shard_map/step0/ppermute | solution.py:427
  73.5 5.9 %collective-permute-start.8 = (bf16[9,16,128]{2,1,0:T(8,128)(2,1)S(1)}, bf16[9,16,128]{2,1,0:T(8,128)(2,1)S(1)}, u32[]{:S(2)}, u32[]{:S(2)}) collective-permute-start(bf16[9,16,128]{2,1,0:T(8,128)(2,1)S(1)} %get-tuple-element.37.refs_2_), channel_id=1, source_target_pairs={{0,32},{16,48},{32,0},{48,16},{64,96},{80,112},{96,64},{112,80},{1... | collective-permute-start | bytes 110600 | tf_op jit(solution)/shard_map/step0/ppermute | solution.py:427
  74.4 5.5 %collective-permute-start.7 = (bf16[9,16,128]{2,1,0:T(8,128)(2,1)S(1)}, bf16[9,16,128]{2,1,0:T(8,128)(2,1)S(1)}, u32[]{:S(2)}, u32[]{:S(2)}) collective-permute-start(bf16[9,16,128]{2,1,0:T(8,128)(2,1)S(1)} %get-tuple-element.37.refs_2_), channel_id=1, source_target_pairs={{0,16},{16,0},{32,48},{48,32},{64,80},{80,64},{96,112},{112,96},{1... | collective-permute-start | bytes 110600 | tf_op jit(solution)/shard_map/step0/ppermute | solution.py:427
  77.1 2.8 %collective-permute-start.13 = (bf16[9,16,128]{2,1,0:T(8,128)(2,1)S(1)}, bf16[9,16,128]{2,1,0:T(8,128)(2,1)S(1)}, u32[]{:S(2)}, u32[]{:S(2)}) collective-permute-start(bf16[9,16,128]{2,1,0:T(8,128)(2,1)S(1)} %collective-permute-done.12.refs_8_), channel_id=1, source_target_pairs={{0,16},{16,0},{32,48},{48,32},{64,80},{80,64},{96,112},{112,96},{1... | collective-permute-start | bytes 110600 | tf_op jit(solution)/shard_map/step0/ppermute | solution.py:427
  78.2 2.1 %collective-permute-start.11 = (bf16[9,16,128]{2,1,0:T(8,128)(2,1)S(1)}, bf16[9,16,128]{2,1,0:T(8,128)(2,1)S(1)}, u32[]{:S(2)}, u32[]{:S(2)}) collective-permute-start(bf16[9,16,128]{2,1,0:T(8,128)(2,1)S(1)} %collective-permute-done.10.refs_6_), channel_id=1, source_target_pairs={{0,16},{16,0},{32,48},{48,32},{64,80},{80,64},{96,112},{112,96},{1... | collective-permute-start | bytes 110600 | tf_op jit(solution)/shard_map/step0/ppermute | solution.py:427
  79.4 1.4 collective-permute-start.9
  103.6 6.0 %collective-permute-start.19 = (bf16[9,16,128]{2,1,0:T(8,128)(2,1)S(1)}, bf16[9,16,128]{2,1,0:T(8,128)(2,1)S(1)}, u32[]{:S(2)}, u32[]{:S(2)}) collective-permute-start(bf16[9,16,128]{2,1,0:T(8,128)(2,1)S(1)} %get-tuple-element.40.refs_2_), channel_id=1, source_target_pairs={{0,96},{16,112},{32,64},{48,80},{64,32},{80,48},{96,0},{112,16},{1... | collective-permute-start | bytes 110600 | tf_op jit(solution)/shard_map/step1/ppermute | solution.py:427
  105.7 5.3 %collective-permute-start.17 = (bf16[9,16,128]{2,1,0:T(8,128)(2,1)S(1)}, bf16[9,16,128]{2,1,0:T(8,128)(2,1)S(1)}, u32[]{:S(2)}, u32[]{:S(2)}) collective-permute-start(bf16[9,16,128]{2,1,0:T(8,128)(2,1)S(1)} %get-tuple-element.40.refs_2_), channel_id=1, source_target_pairs={{0,64},{16,80},{32,96},{48,112},{64,0},{80,16},{96,32},{112,48},{1... | collective-permute-start | bytes 110600 | tf_op jit(solution)/shard_map/step1/ppermute | solution.py:427
  106.4 6.7 %collective-permute-start.15 = (bf16[9,16,128]{2,1,0:T(8,128)(2,1)S(1)}, bf16[9,16,128]{2,1,0:T(8,128)(2,1)S(1)}, u32[]{:S(2)}, u32[]{:S(2)}) collective-permute-start(bf16[9,16,128]{2,1,0:T(8,128)(2,1)S(1)} %get-tuple-element.40.refs_2_), channel_id=1, source_target_pairs={{0,32},{16,48},{32,0},{48,16},{64,96},{80,112},{96,64},{112,80},{1... | collective-permute-start | bytes 110600 | tf_op jit(solution)/shard_map/step1/ppermute | solution.py:427
  106.9 6.2 %collective-permute-start.14 = (bf16[9,16,128]{2,1,0:T(8,128)(2,1)S(1)}, bf16[9,16,128]{2,1,0:T(8,128)(2,1)S(1)}, u32[]{:S(2)}, u32[]{:S(2)}) collective-permute-start(bf16[9,16,128]{2,1,0:T(8,128)(2,1)S(1)} %get-tuple-element.40.refs_2_), channel_id=1, source_target_pairs={{0,16},{16,0},{32,48},{48,32},{64,80},{80,64},{96,112},{112,96},{1... | collective-permute-start | bytes 110600 | tf_op jit(solution)/shard_map/step1/ppermute | solution.py:427
  109.5 3.6 %collective-permute-start.20 = (bf16[9,16,128]{2,1,0:T(8,128)(2,1)S(1)}, bf16[9,16,128]{2,1,0:T(8,128)(2,1)S(1)}, u32[]{:S(2)}, u32[]{:S(2)}) collective-permute-start(bf16[9,16,128]{2,1,0:T(8,128)(2,1)S(1)} %collective-permute-done.19.refs_8_), channel_id=1, source_target_pairs={{0,16},{16,0},{32,48},{48,32},{64,80},{80,64},{96,112},{112,96},{1... | collective-permute-start | bytes 110600 | tf_op jit(solution)/shard_map/step1/ppermute | solution.py:427
  111.0 2.9 %collective-permute-start.18 = (bf16[9,16,128]{2,1,0:T(8,128)(2,1)S(1)}, bf16[9,16,128]{2,1,0:T(8,128)(2,1)S(1)}, u32[]{:S(2)}, u32[]{:S(2)}) collective-permute-start(bf16[9,16,128]{2,1,0:T(8,128)(2,1)S(1)} %collective-permute-done.17.refs_6_), channel_id=1, source_target_pairs={{0,16},{16,0},{32,48},{48,32},{64,80},{80,64},{96,112},{112,96},{1... | collective-permute-start | bytes 110600 | tf_op jit(solution)/shard_map/step1/ppermute | solution.py:427
  113.1 1.2 collective-permute-start.16
  137.4 5.8 %collective-permute-start.26 = (bf16[9,16,128]{2,1,0:T(8,128)(2,1)S(1)}, bf16[9,16,128]{2,1,0:T(8,128)(2,1)S(1)}, u32[]{:S(2)}, u32[]{:S(2)}) collective-permute-start(bf16[9,16,128]{2,1,0:T(8,128)(2,1)S(1)} %get-tuple-element.44.refs_2_), channel_id=1, source_target_pairs={{0,96},{16,112},{32,64},{48,80},{64,32},{80,48},{96,0},{112,16},{1... | collective-permute-start | bytes 110600 | tf_op jit(solution)/shard_map/step2/ppermute | solution.py:427
  138.3 6.0 %collective-permute-start.24 = (bf16[9,16,128]{2,1,0:T(8,128)(2,1)S(1)}, bf16[9,16,128]{2,1,0:T(8,128)(2,1)S(1)}, u32[]{:S(2)}, u32[]{:S(2)}) collective-permute-start(bf16[9,16,128]{2,1,0:T(8,128)(2,1)S(1)} %get-tuple-element.44.refs_2_), channel_id=1, source_target_pairs={{0,64},{16,80},{32,96},{48,112},{64,0},{80,16},{96,32},{112,48},{1... | collective-permute-start | bytes 110600 | tf_op jit(solution)/shard_map/step2/ppermute | solution.py:427
  139.0 6.7 %collective-permute-start.22 = (bf16[9,16,128]{2,1,0:T(8,128)(2,1)S(1)}, bf16[9,16,128]{2,1,0:T(8,128)(2,1)S(1)}, u32[]{:S(2)}, u32[]{:S(2)}) collective-permute-start(bf16[9,16,128]{2,1,0:T(8,128)(2,1)S(1)} %get-tuple-element.44.refs_2_), channel_id=1, source_target_pairs={{0,32},{16,48},{32,0},{48,16},{64,96},{80,112},{96,64},{112,80},{1... | collective-permute-start | bytes 110600 | tf_op jit(solution)/shard_map/step2/ppermute | solution.py:427
  140.7 4.9 %collective-permute-start.21 = (bf16[9,16,128]{2,1,0:T(8,128)(2,1)S(1)}, bf16[9,16,128]{2,1,0:T(8,128)(2,1)S(1)}, u32[]{:S(2)}, u32[]{:S(2)}) collective-permute-start(bf16[9,16,128]{2,1,0:T(8,128)(2,1)S(1)} %get-tuple-element.44.refs_2_), channel_id=1, source_target_pairs={{0,16},{16,0},{32,48},{48,32},{64,80},{80,64},{96,112},{112,96},{1... | collective-permute-start | bytes 110600 | tf_op jit(solution)/shard_map/step2/ppermute | solution.py:427
  143.2 2.4 %collective-permute-start.27 = (bf16[9,16,128]{2,1,0:T(8,128)(2,1)S(1)}, bf16[9,16,128]{2,1,0:T(8,128)(2,1)S(1)}, u32[]{:S(2)}, u32[]{:S(2)}) collective-permute-start(bf16[9,16,128]{2,1,0:T(8,128)(2,1)S(1)} %collective-permute-done.26.refs_8_), channel_id=1, source_target_pairs={{0,16},{16,0},{32,48},{48,32},{64,80},{80,64},{96,112},{112,96},{1... | collective-permute-start | bytes 110600 | tf_op jit(solution)/shard_map/step2/ppermute | solution.py:427
  144.3 2.2 %collective-permute-start.25 = (bf16[9,16,128]{2,1,0:T(8,128)(2,1)S(1)}, bf16[9,16,128]{2,1,0:T(8,128)(2,1)S(1)}, u32[]{:S(2)}, u32[]{:S(2)}) collective-permute-start(bf16[9,16,128]{2,1,0:T(8,128)(2,1)S(1)} %collective-permute-done.24.refs_6_), channel_id=1, source_target_pairs={{0,16},{16,0},{32,48},{48,32},{64,80},{80,64},{96,112},{112,96},{1... | collective-permute-start | bytes 110600 | tf_op jit(solution)/shard_map/step2/ppermute | solution.py:427
  145.6 1.2 collective-permute-start.23
